TPU v7x, 512 devices: a whole 4x4x16 slice. The times are simulated.
512 devices in a mesh: dom: 64 (over y_hi, z, core), epoch: 8 (over x, y_lo).
Axes of the slice: x: 4, y: 4 (y_hi: 2, y_lo: 2; y = y_hi * 2 + y_lo), z: 16, core: 2. Of those that a mesh axis runs over, the one named last changes fastest.
Arguments:
- memory: bfloat16 [8, 32768, 256], P('epoch', 'dom'), may hold values from -6 to 6
- neighbours: int32 [32768, 10], P('dom'), may hold values from 0 to 511
- owners: int32 [8, 8192, 2], P('epoch', 'dom'), may hold values from 0 to 63, all different within a row; in each aligned block of 128 rows (0 to 127, 128 to 255, ..., all dimensions but the last counted through in order) at most 8 rows name the same one
- rows: int32 [8, 8192, 2], P('epoch', 'dom'), may hold values from 0 to 511
- edge_feat: bfloat16 [8, 8192, 128], P('epoch', 'dom'), may hold values from -24 to 24
- labels: int32 [8, 8192], P('epoch', 'dom'), may hold values 0 or 1
- w_query: bfloat16 [256, 256], replicated, may hold values from -0.375 to 0.375
- w_keyval: bfloat16 [256, 512], replicated, may hold values from -0.375 to 0.375
- w_out: bfloat16 [256, 256], replicated, may hold values from -0.375 to 0.375
- w_msg_mem: bfloat16 [256, 256], replicated, may hold values from -0.375 to 0.375
- w_msg_edge: bfloat16 [128, 256], replicated, may hold values from -0.5 to 0.5
- w_pair_edge: bfloat16 [128, 256], replicated, may hold values from -0.5 to 0.5
- gru_input: bfloat16 [256, 768], replicated, may hold values from -0.375 to 0.375
- gru_hidden: bfloat16 [256, 768], replicated, may hold values from -0.375 to 0.375
- gru_bias: float32 [768], replicated, may hold values from -0.5 to 0.5
- bn_gain: float32 [256], replicated, may hold values from 0.1 to 1.9
- bn_shift: float32 [256], replicated, may hold values from -3 to 3
- w_score: bfloat16 [256], replicated, may hold values from -1 to 1
Outputs:
- new_memory: bfloat16 [8, 32768, 256], P('epoch', 'dom')
- loss: float32 [8], P('epoch')
Inputs may be any that keep to these rules, and one draw needn't show every extreme that they name: Within the 128 events of one device, no partition owns more than 8 endpoints, and some partition owns exactly 8; an event's two endpoints have different owners.
All inputs are finite; a program needn't handle non-finite values. No bound on the sum of `labels` on one device may be relied on, other than what follows from the above.
Results may differ from a plain program's by a relative error of at most 0.001.
The roundings to bfloat16 on the way count: a program that leaves them out, or rounds other values in their place, can miss the bound.
Values may be sent and summed in bfloat16 or wider, within the bound.
A program may use at most 64 MiB of HBM per device.

v0:
```python
import jax
import jax.numpy as jnp
from jax import lax
from jax.sharding import PartitionSpec as P


def passed_along(shard, axis, by):
    devices = lax.axis_size(axis)
    pairs = [(i, i + by) for i in range(devices) if 0 <= i + by < devices]
    return lax.ppermute(shard, axis, pairs)


def gru(avg, hidden, gru_input, gru_hidden, gru_bias):
    width = hidden.shape[1]
    inp = jnp.dot(avg, gru_input, preferred_element_type=jnp.float32) + gru_bias
    hid = jnp.dot(hidden, gru_hidden, preferred_element_type=jnp.float32)
    reset = jax.nn.sigmoid(inp[:, :width] + hid[:, :width])
    update = jax.nn.sigmoid(inp[:, width : 2 * width] + hid[:, width : 2 * width])
    cand = jnp.tanh(inp[:, 2 * width :] + reset * hid[:, 2 * width :])
    return ((1.0 - update) * cand + update * hidden.astype(jnp.float32)).astype(jnp.bfloat16)


def shards(
    memory,
    neighbours,
    owners,
    rows,
    edge_feat,
    labels,
    w_query,
    w_keyval,
    w_out,
    w_msg_mem,
    w_msg_edge,
    w_pair_edge,
    gru_input,
    gru_hidden,
    gru_bias,
    bn_gain,
    bn_shift,
    w_score,
):
    parts = lax.axis_size("dom")
    table = memory[0]
    nodes = table.shape[0]
    width = table.shape[1]
    events = owners.shape[1]
    slots = 4 * events // parts
    heads = 2
    hsize = width // heads
    keyval = jnp.dot(table, w_keyval, preferred_element_type=jnp.float32).astype(jnp.bfloat16)
    owner_flat = owners[0].reshape(-1)
    local_flat = rows[0].reshape(-1)
    onehot = (owner_flat[:, None] == jnp.arange(parts, dtype=jnp.int32)[None, :]).astype(jnp.int32)
    before = jnp.cumsum(onehot, axis=0) - onehot
    place = owner_flat * slots + jnp.sum(before * onehot, axis=1)
    request = (
        jnp.full((parts * slots,), -1, jnp.int32).at[place].set(local_flat).reshape(parts, slots)
    )
    received = lax.all_to_all(request, "dom", split_axis=0, concat_axis=0, tiled=True)
    valid = received >= 0
    safe = jnp.where(valid, received, 0)
    mrow = table[safe]
    query = jnp.dot(mrow, w_query, preferred_element_type=jnp.float32).astype(jnp.bfloat16)
    gathered = keyval[neighbours[safe]]
    src, cnt = received.shape
    keys = gathered[..., :width].reshape(src, cnt, -1, heads, hsize)
    values = gathered[..., width:].reshape(src, cnt, -1, heads, hsize)
    qh = query.reshape(src, cnt, heads, hsize)
    scores = jnp.einsum(
        "abhd,abjhd->abhj", qh, keys, preferred_element_type=jnp.float32
    ) / jnp.sqrt(jnp.float32(hsize))
    probs = jax.nn.softmax(scores, axis=-1).astype(jnp.bfloat16)
    attended = (
        jnp.einsum("abhj,abjhd->abhd", probs, values, preferred_element_type=jnp.float32)
        .astype(jnp.bfloat16)
        .reshape(src, cnt, width)
    )
    embed = (
        mrow.astype(jnp.float32) + jnp.dot(attended, w_out, preferred_element_type=jnp.float32)
    ).astype(jnp.bfloat16)
    back_embed = lax.all_to_all(embed, "dom", split_axis=0, concat_axis=0, tiled=True)
    back_rows = lax.all_to_all(mrow, "dom", split_axis=0, concat_axis=0, tiled=True)
    embed = back_embed.reshape(-1, width)[place].reshape(events, 2, width)
    mrows = back_rows.reshape(-1, width)[place].reshape(events, 2, width)
    feat = edge_feat[0]
    pair = embed[:, 0].astype(jnp.float32) * embed[:, 1].astype(jnp.float32) + jnp.dot(
        feat, w_pair_edge, preferred_element_type=jnp.float32
    )
    sum_one, sum_two = lax.psum((jnp.sum(pair, axis=0), jnp.sum(pair * pair, axis=0)), "dom")
    total = jnp.float32(events * parts)
    mean = sum_one / total
    var = sum_two / total - mean * mean
    normed = (pair - mean) * lax.rsqrt(var + 1e-05) * bn_gain + bn_shift
    logit = jnp.dot(
        jax.nn.relu(normed), w_score.astype(jnp.float32), precision=lax.Precision.HIGHEST
    )
    terms = jax.nn.softplus(logit) - labels[0].astype(jnp.float32) * logit
    loss = lax.psum(jnp.sum(terms), "dom") / total
    other = mrows[:, ::-1]
    message = (
        (
            jnp.dot(other, w_msg_mem, preferred_element_type=jnp.float32)
            + jnp.dot(feat, w_msg_edge, preferred_element_type=jnp.float32)[:, None, :]
        )
        .astype(jnp.bfloat16)
        .reshape(-1, width)
    )
    outbox = (
        jnp.zeros((parts * slots, width), jnp.bfloat16)
        .at[place]
        .set(message)
        .reshape(parts, slots, width)
    )
    inbox = lax.all_to_all(outbox, "dom", split_axis=0, concat_axis=0, tiled=True).reshape(
        -1, width
    )
    ids = received.reshape(-1)
    valid = ids >= 0
    safe = jnp.where(valid, ids, 0)
    agg = (
        jnp.zeros((nodes, width), jnp.float32)
        .at[safe]
        .add(jnp.where(valid[:, None], inbox.astype(jnp.float32), 0.0))
    )
    count = jnp.zeros((nodes,), jnp.float32).at[safe].add(valid.astype(jnp.float32))
    avg = (agg[safe] / jnp.maximum(count[safe], 1.0)[:, None]).astype(jnp.bfloat16)
    fresh = gru(avg, table[safe], gru_input, gru_hidden, gru_bias)
    target = jnp.where(valid, ids, nodes)
    updated = table.at[target].set(fresh, mode="drop")
    touched = jnp.zeros((nodes,), jnp.float32).at[target].set(1.0, mode="drop")
    prev_rows, prev_touched = (
        passed_along(updated, "epoch", 1),
        passed_along(touched.astype(jnp.bfloat16), "epoch", 1).astype(touched.dtype),
    )
    prior = jnp.where(prev_touched[:, None] > 0, prev_rows, table)
    result = jnp.where(touched[:, None] > 0, updated, prior)
    return (result[None], loss.reshape(1))


def solution(mesh):
    return jax.shard_map(
        shards,
        mesh=mesh,
        in_specs=(
            P("epoch", "dom", None),
            P("dom", None),
            P("epoch", "dom", None),
            P("epoch", "dom", None),
            P("epoch", "dom", None),
            P("epoch", "dom"),
            P(),
            P(),
            P(),
            P(),
            P(),
            P(),
            P(),
            P(),
            P(),
            P(),
            P(),
            P(),
        ),
        out_specs=(P("epoch", "dom", None), P("epoch")),
        check_vma=False,
    )
```

profile of v0, /device:TPU:1, one launch (start us, length us, event | category | flops | bytes accessed | tf_op | source)
XLA Modules:
  0.0 454.2 jit_solution(15380148399347106963)
XLA Ops:
  0.6 0.8 copy.48
  1.8 0.7 broadcast_multiply_fusion.1
  2.5 0.6 reduce-window.6
  3.6 0.8 copy.51
  4.6 1.4 scatter_custom_fusion
  6.0 0.7 all_to_all.17
  6.7 19.8 %all-to-all-start = ((s32[64,1,8]{2,1,0:T(1,128)}), s32[64,1,8]{2,1,0:T(1,128)S(1)}, u32[]{:S(2)}, u32[]{:S(2)}) async-start(s32[64,1,8]{2,1,0:T(1,128)} %bitcast.3), calls=%async_computation | async-start | bytes 65536 | tf_op jit(solution)/shard_map/all_to_all | solution.py:60
  26.5 1.3 convolution_convert_fusion
  27.8 0.9 copy.55
  28.7 12.5 %all-to-all-done = s32[64,1,8]{2,1,0:T(1,128)S(1)} async-done(((s32[64,1,8]{2,1,0:T(1,128)}), s32[64,1,8]{2,1,0:T(1,128)S(1)}, u32[]{:S(2)}, u32[]{:S(2)}) %all-to-all-start) | async-done | bytes 2080 | tf_op jit(solution)/shard_map/all_to_all | solution.py:60
  41.3 1.0 gather_fusion.5
  42.6 21.4 %gather_fusion.6 = bf16[5120,512]{1,0:T(8,128)(2,1)} fusion(bf16[512,512]{1,0:T(8,128)(2,1)S(1)} %convolution_convert_fusion, s32[5120]{0:T(1024)S(1)} %broadcast_clamp_fusion), kind=kCustom, calls=%fused_computation.6 | custom fusion | bytes 10506240 | tf_op jit(solution)/shard_map/gather | solution.py:65
  63.9 10.5 %reshape.274 = bf16[64,8,10,512]{3,2,1,0:T(8,128)(2,1)} reshape(bf16[5120,512]{1,0:T(8,128)(2,1)} %gather_fusion.6) | data formatting | bytes 10485760 | tf_op jit(solution)/shard_map/gather | solution.py:65
  74.4 6.0 %fusion.70 = (bf16[64,8,10,256]{3,2,1,0:T(8,128)(2,1)}, bf16[64,8,10,256]{3,2,1,0:T(8,128)(2,1)}) fusion(bf16[64,8,10,512]{3,2,1,0:T(8,128)(2,1)} %reshape.274), kind=kLoop, calls=%fused_computation.124 | loop fusion | bytes 10485760 | tf_op jit(solution)/shard_map/slice | solution.py:68
  80.4 2.6 gather_fusion
  83.0 10.3 %copy_bitcast_fusion = (bf16[64,8,10,2,128]{4,1,3,2,0:T(8,128)(2,1)}, bf16[64,8,10,2,128]{4,1,3,2,0:T(8,128)(2,1)S(1)}) fusion(bf16[64,8,10,256]{3,2,1,0:T(8,128)(2,1)} %get-tuple-element.6, bf16[64,8,10,256]{3,2,1,0:T(8,128)(2,1)} %get-tuple-element.7), kind=kLoop, calls=%fused_computation.18 | loop fusion | bytes 10485760 | tf_op jit(solution)/shard_map/reshape | solution.py:68
  93.3 1.2 fusion.5
  94.5 2.3 fusion.2
  96.7 0.7 copy.62
  97.4 4.7 %all-to-all-start.1 = ((bf16[64,8,256]{2,1,0:T(8,128)(2,1)}), bf16[64,8,256]{2,1,0:T(8,128)(2,1)S(1)}, u32[]{:S(2)}, u32[]{:S(2)}) async-start(bf16[64,8,256]{2,1,0:T(8,128)(2,1)} %bitcast.8), calls=%async_computation.1 | async-start | bytes 524288 | tf_op jit(solution)/shard_map/all_to_all | solution.py:83
  102.2 0.9 copy.63
  103.1 3.1 fusion
  106.2 1.9 fusion.4
  108.1 17.8 %all-to-all-done.1 = bf16[64,8,256]{2,1,0:T(8,128)(2,1)S(1)} async-done(((bf16[64,8,256]{2,1,0:T(8,128)(2,1)}), bf16[64,8,256]{2,1,0:T(8,128)(2,1)S(1)}, u32[]{:S(2)}, u32[]{:S(2)}) %all-to-all-start.1) | async-done | bytes 262176 | tf_op jit(solution)/shard_map/all_to_all | solution.py:83
  125.9 4.2 all-to-all-start.3
  131.4 0.7 reduce.7
  132.5 4.1 scatter_custom_fusion.4
  136.6 3.5 gather_fusion.3
  140.1 2.4 scatter_custom_fusion.1
  143.1 1.2 gather_fusion.1
  144.8 2.1 scatter_custom_fusion.2
  147.0 6.8 %all-to-all-done.3 = bf16[64,8,256]{2,1,0:T(8,128)(2,1)S(1)} async-done(((bf16[64,8,256]{2,1,0:T(8,128)(2,1)}), bf16[64,8,256]{2,1,0:T(8,128)(2,1)S(1)}, u32[]{:S(2)}, u32[]{:S(2)}) %all-to-all-start.3) | async-done | bytes 262176 | tf_op jit(solution)/shard_map/all_to_all | solution.py:82
  153.7 8.3 %all-to-all-start.2 = ((bf16[64,8,256]{2,1,0:T(8,128)(2,1)}), bf16[64,8,256]{2,1,0:T(8,128)(2,1)S(1)}, u32[]{:S(2)}, u32[]{:S(2)}) async-start(bf16[64,8,256]{2,1,0:T(8,128)(2,1)} %bitcast.12), calls=%async_computation.2 | async-start | bytes 524288 | tf_op jit(solution)/shard_map/all_to_all | solution.py:115
  162.5 1.9 gather_fusion.4
  165.1 2.9 collective-permute-start
  168.3 1.2 gather_fusion.7
  169.8 0.8 fusion.69
  170.6 129.9 %all-reduce = (f32[256]{0:T(256)S(1)}, f32[256]{0:T(256)S(1)}) all-reduce(f32[256]{0:T(256)S(1)} %get-tuple-element.3, f32[256]{0:T(256)S(1)} %get-tuple-element.2), channel_id=1, replica_groups=mesh['dom'=64,'epoch'=8] {'dom'}, use_global_device_ids=true, to_apply=%region_14.15 | all-reduce | flops 512 | bytes 4096 | tf_op jit(solution)/shard_map/psum | solution.py:90
  300.5 0.6 broadcast_multiply_fusion
  301.1 3.6 scatter_custom_fusion.3
  304.7 2.2 gather_fusion.2
  307.0 2.8 convolution_add_fusion
  309.8 3.6 scatter_custom_fusion.5
  313.4 2.5 collective-permute-start.1
  316.0 0.8 fusion.63
  316.8 0.7 convert_compare_fusion
  317.5 134.0 %psum.23 = f32[]{:T(128)} all-reduce(f32[]{:T(128)} %fusion.63), channel_id=1, replica_groups=mesh['dom'=64,'epoch'=8] {'dom'}, use_global_device_ids=true, to_apply=%region_16.17 | all-reduce | flops 1 | bytes 8 | tf_op jit(solution)/shard_map/psum | solution.py:99
  452.2 0.9 select_bitcast_fusion
  (87 shorter events, 5.8 us)
Async XLA Ops:
  0.6 167.3 %copy-start = (bf16[256,768]{1,0:T(8,128)(2,1)S(1)}, bf16[256,768]{1,0:T(8,128)(2,1)}, u32[]{:S(2)}) copy-start(bf16[256,768]{1,0:T(8,128)(2,1)} %param.31) | copy-start | bytes 1179652
  6.7 34.5 %all-to-all-start = ((s32[64,1,8]{2,1,0:T(1,128)}), s32[64,1,8]{2,1,0:T(1,128)S(1)}, u32[]{:S(2)}, u32[]{:S(2)}) async-start(s32[64,1,8]{2,1,0:T(1,128)} %bitcast.3), calls=%async_computation | async-start | bytes 65536 | tf_op jit(solution)/shard_map/all_to_all | solution.py:60
  74.4 6.0 %copy-start.1 = (bf16[1,512,256]{2,1,0:T(8,128)(2,1)S(1)}, bf16[1,512,256]{2,1,0:T(8,128)(2,1)}, u32[]{:S(2)}) copy-start(bf16[1,512,256]{2,1,0:T(8,128)(2,1)} %param.18) | copy-start | bytes 786436
  83.0 10.3 %copy-start.2 = (bf16[256,256]{1,0:T(8,128)(2,1)S(1)}, bf16[256,256]{1,0:T(8,128)(2,1)}, u32[]{:S(2)}) copy-start(bf16[256,256]{1,0:T(8,128)(2,1)} %param.24) | copy-start | bytes 393220
  97.4 28.5 %all-to-all-start.1 = ((bf16[64,8,256]{2,1,0:T(8,128)(2,1)}), bf16[64,8,256]{2,1,0:T(8,128)(2,1)S(1)}, u32[]{:S(2)}, u32[]{:S(2)}) async-start(bf16[64,8,256]{2,1,0:T(8,128)(2,1)} %bitcast.8), calls=%async_computation.1 | async-start | bytes 524288 | tf_op jit(solution)/shard_map/all_to_all | solution.py:83
  103.1 3.1 copy-start.3
  103.1 27.0 %copy-start.6 = (bf16[1,128,128]{2,1,0:T(8,128)(2,1)S(1)}, bf16[1,128,128]{2,1,0:T(8,128)(2,1)}, u32[]{:S(2)}) copy-start(bf16[1,128,128]{2,1,0:T(8,128)(2,1)} %param.22) | copy-start | bytes 98308
  103.1 27.0 %copy-start.8 = (bf16[128,256]{1,0:T(8,128)(2,1)S(1)}, bf16[128,256]{1,0:T(8,128)(2,1)}, u32[]{:S(2)}) copy-start(bf16[128,256]{1,0:T(8,128)(2,1)} %param.28) | copy-start | bytes 196612
  103.1 27.2 %copy-start.17 = (bf16[256]{0:T(256)(128)(2,1)S(1)}, bf16[256]{0:T(256)(128)(2,1)}, u32[]{:S(2)}) copy-start(bf16[256]{0:T(256)(128)(2,1)} %param.35) | copy-start | bytes 1540
  125.9 27.8 %all-to-all-start.3 = ((bf16[64,8,256]{2,1,0:T(8,128)(2,1)}), bf16[64,8,256]{2,1,0:T(8,128)(2,1)S(1)}, u32[]{:S(2)}, u32[]{:S(2)}) async-start(bf16[64,8,256]{2,1,0:T(8,128)(2,1)} %fusion.4), calls=%async_computation.3 | async-start | bytes 524288 | tf_op jit(solution)/shard_map/all_to_all | solution.py:82
  130.1 14.3 %copy-start.4 = (bf16[256,256]{1,0:T(8,128)(2,1)S(1)}, bf16[256,256]{1,0:T(8,128)(2,1)}, u32[]{:S(2)}) copy-start(bf16[256,256]{1,0:T(8,128)(2,1)} %param.27) | copy-start | bytes 393220
  132.5 10.6 %copy-start.11 = (s32[512,1]{0,1:T(1,128)}, s32[512,1]{0,1:T(1,128)S(1)}, u32[]{:S(2)}) copy-start(s32[512,1]{0,1:T(1,128)S(1)} %get-tuple-element.11) | copy-start | bytes 6148
  153.7 147.4 %all-to-all-start.2 = ((bf16[64,8,256]{2,1,0:T(8,128)(2,1)}), bf16[64,8,256]{2,1,0:T(8,128)(2,1)S(1)}, u32[]{:S(2)}, u32[]{:S(2)}) async-start(bf16[64,8,256]{2,1,0:T(8,128)(2,1)} %bitcast.12), calls=%async_computation.2 | async-start | bytes 524288 | tf_op jit(solution)/shard_map/all_to_all | solution.py:115
  164.5 5.3 %copy-start.7 = (bf16[1,128,128]{2,1,0:T(8,128)(2,1)S(1)}, bf16[1,128,128]{2,1,0:T(8,128)(2,1)}, u32[]{:S(2)}) copy-start(bf16[1,128,128]{2,1,0:T(8,128)(2,1)} %param.22) | copy-start | bytes 98308
  164.5 5.3 %copy-start.9 = (bf16[128,256]{1,0:T(8,128)(2,1)S(1)}, bf16[128,256]{1,0:T(8,128)(2,1)}, u32[]{:S(2)}) copy-start(bf16[128,256]{1,0:T(8,128)(2,1)} %param.29) | copy-start | bytes 196612
  165.1 151.7 %collective-permute-start = (bf16[512]{0:T(512)(128)(2,1)}, bf16[512]{0:T(512)(128)(2,1)}, u32[]{:S(2)}, u32[]{:S(2)}) collective-permute-start(bf16[512]{0:T(512)(128)(2,1)} %convert_element_type.76), channel_id=1, source_target_pairs={{0,1},{1,2},{2,3},{3,4},{4,5},{5,6},{6,7},{8,9},{9,10},{10,11},{11... | collective-permute-start | bytes 3080 | tf_op jit(solution)/shard_map/ppermute | solution.py:10
  301.1 5.8 %copy-start.12 = (f32[512]{0:T(512)S(1)}, f32[512]{0:T(512)}, u32[]{:S(2)}) copy-start(f32[512]{0:T(512)} %broadcast_maximum_fusion) | copy-start | bytes 6148
  307.0 9.0 %copy-start.5 = (f32[128,256]{1,0:T(8,128)S(1)}, f32[128,256]{1,0:T(8,128)}, u32[]{:S(2)}) copy-start(f32[128,256]{1,0:T(8,128)} %get-tuple-element.14) | copy-start | bytes 393220
  307.0 9.0 %copy-start.13 = (f32[256]{0:T(256)S(1)}, f32[256]{0:T(256)}, u32[]{:S(2)}) copy-start(f32[256]{0:T(256)} %get-tuple-element.12) | copy-start | bytes 3076
  307.0 9.0 %copy-start.14 = (f32[256]{0:T(256)S(1)}, f32[256]{0:T(256)}, u32[]{:S(2)}) copy-start(f32[256]{0:T(256)} %get-tuple-element.13) | copy-start | bytes 3076
  307.0 9.0 %copy-start.15 = (f32[256]{0:T(256)S(1)}, f32[256]{0:T(256)}, u32[]{:S(2)}) copy-start(f32[256]{0:T(256)} %param.34) | copy-start | bytes 3076
  307.0 9.0 %copy-start.16 = (f32[256]{0:T(256)S(1)}, f32[256]{0:T(256)}, u32[]{:S(2)}) copy-start(f32[256]{0:T(256)} %param.33) | copy-start | bytes 3076
  307.0 9.0 %copy-start.18 = (s32[1,128]{1,0:T(1,128)S(1)}, s32[1,128]{1,0:T(1,128)}, u32[]{:S(2)}) copy-start(s32[1,128]{1,0:T(1,128)} %param.23) | copy-start | bytes 1540
  307.0 9.0 %copy-start.19 = (bf16[256,1]{0,1:T(2,128)(2,1)S(1)}, bf16[256,1]{0,1:T(2,128)(2,1)}, u32[]{:S(2)}) copy-start(bf16[256,1]{0,1:T(2,128)(2,1)} %reshape.348) | copy-start | bytes 1540
  307.0 145.2 %copy-start.10 = (pred[512]{0:T(512)(128)(4,1)S(1)}, pred[512]{0:T(512)(128)(4,1)}, u32[]{:S(2)}) copy-start(pred[512]{0:T(512)(128)(4,1)} %broadcast_compare_fusion) | copy-start | bytes 1540
  313.4 138.7 %collective-permute-start.1 = (bf16[512,256]{1,0:T(8,128)(2,1)S(1)}, bf16[512,256]{1,0:T(8,128)(2,1)S(1)}, u32[]{:S(2)}, u32[]{:S(2)}) collective-permute-start(bf16[512,256]{1,0:T(8,128)(2,1)S(1)} %scatter_custom_fusion.5), channel_id=1, source_target_pairs={{0,1},{1,2},{2,3},{3,4},{4,5},{5,6},{6,7},{8,9},{9,10},{10,11},{11... | collective-permute-start | bytes 786440 | tf_op jit(solution)/shard_map/ppermute | solution.py:10
where the time goes:
time: 455 us; the launch traced here: 454 us
  blocking collectives  264 us (58%)
  local copies, waits for them, and re-layouts  75.5 us (17%)
  starting transfers between devices  42.3 us (9%)
  waiting for transfers between devices  37.1 us (8%)
  other arithmetic  17.6 us (4%)
  matrix products  14.8 us (3%)
    psum x1, blocking collectives, shards(): loss = lax.psum(jnp.sum(terms), 'dom') / total  134 us
    psum x1, blocking collectives, shards(): lax.psum((jnp.sum(pair, axis=0), jnp.sum(pair * pair, axis=0)), 'dom')  130 us
    gather x3, local copies, waits for them, and re-layouts, shards(): gathered = keyval[neighbours[safe]]  32.9 us
    all_to_all x1, starting transfers between devices, shards(): lax.all_to_all(request, 'dom', split_axis=0, concat_axis=0, tiled=True)  19.8 us
    all_to_all x1, waiting for transfers between devices, shards(): lax.all_to_all(mrow, 'dom', split_axis=0, concat_axis=0, tiled=True)  17.8 us
    all_to_all x1, waiting for transfers between devices, shards(): lax.all_to_all(request, 'dom', split_axis=0, concat_axis=0, tiled=True)  12.5 us
    reshape x1, local copies, waits for them, and re-layouts, shards(): values = gathered[..., width:].reshape(src, cnt, -1, heads, hsize)  10.3 us
  transfers between devices with their start and end apart: 6, of which 3 were waited for; matrix products, arithmetic and copies ran while one was open for 10% of the time, Pallas kernels for 0%

commit v1 on v0

v1 whole, which is shorter than its diff:
```python
import functools

import jax
import jax.numpy as jnp
from jax import lax
from jax.experimental import pallas as pl
from jax.experimental.pallas import tpu as pltpu
from jax.sharding import PartitionSpec as P

MESH = pl.DeviceIdType.MESH
F32 = jnp.float32
BF16 = jnp.bfloat16
CAP = 8
HEADS = 2
LANES = 128
CORES = 2
HALVES = 2
PLANE = CORES * HALVES
UNTOUCHED = 1e30
NODE_CHUNKS = 4


def iota(shape, dim):
    return lax.broadcasted_iota(jnp.int32, shape, dim)


def dot(a, b):
    return jnp.dot(a, b, preferred_element_type=F32)


def dot_nt(a, b):
    return lax.dot_general(a, b, (((1,), (1,)), ((), ())), preferred_element_type=F32)


def dot_tn(a, b):
    return lax.dot_general(a, b, (((0,), (0,)), ((), ())), preferred_element_type=F32)


def onehot(mask):
    return jnp.where(mask, 1.0, 0.0).astype(BF16)


def pack(x):
    rows = x.shape[0] // CAP
    left = x[:, :LANES].reshape(rows, CAP, LANES)
    right = x[:, LANES:].reshape(rows, CAP, LANES)
    return jnp.concatenate([left, right], axis=1).astype(BF16)


def unpack(x):
    rows = x.shape[0]
    x = x.astype(F32)
    left = x[:, :CAP].reshape(rows * CAP, LANES)
    right = x[:, CAP:].reshape(rows * CAP, LANES)
    return jnp.concatenate([left, right], axis=1).astype(BF16)


def peer_at(me, step, parts):
    rings = parts // PLANE
    step = step + jnp.where(step >= parts - PLANE, 1, 0)
    turn, inside = step // PLANE, step % PLANE
    half = (turn + 1) // 2
    along = rings // 2 + jnp.where(turn % 2 == 1, half, rings - half)
    y, rest = me // (rings * CORES), me % (rings * CORES)
    z, core = rest // CORES, rest % CORES
    spot = (y * CORES + core + inside) % PLANE
    return (spot // CORES) * (rings * CORES) + ((z + along) % rings) * CORES + spot % CORES


def plane_peer(me, by, parts):
    rings = parts // PLANE
    y, rest = me // (rings * CORES), me % (rings * CORES)
    z, core = rest // CORES, rest % CORES
    spot = (y * CORES + core + by) % PLANE
    return (spot // CORES) * (rings * CORES) + z * CORES + spot % CORES


def kernel(
    parts,
    groups,
    table,
    nbr,
    own,
    row,
    feat,
    lab,
    w_query,
    w_keyval,
    w_out,
    w_msg_mem,
    w_msg_edge,
    w_pair_edge,
    gru_input,
    gru_hidden,
    gru_bias,
    bn_gain,
    bn_shift,
    w_score,
    out,
    loss,
    req_s,
    req_r,
    mem_s,
    mem_r,
    emb_s,
    emb_r,
    msg_s,
    msg_r,
    st_s,
    st_r,
    tot_s,
    tot_r,
    ls_s,
    ls_r,
    hand_s,
    hand_r,
    keyval,
    query,
    attended,
    embed,
    hidden,
    pick,
    pick_t,
    place_s,
    place_t,
    send_sem,
    recv_sem,
    st_send,
    st_recv,
    hand_send,
    hand_recv,
):
    me = lax.axis_index("dom")
    group = lax.axis_index("epoch")
    after = lax.rem(group + 1, groups)
    ahead = lax.rem(group + groups - 1, groups)
    nodes, width = table.shape
    events = feat.shape[0]
    slots = parts * CAP
    hsize = width // HEADS

    barrier = pltpu.get_barrier_semaphore()

    def greet(step, carry):
        pl.semaphore_signal(
            barrier, inc=1, device_id={"dom": peer_at(me, step, parts)}, device_id_type=MESH
        )
        return carry

    lax.fori_loop(0, parts - 1, greet, 0)
    pl.semaphore_signal(barrier, inc=1, device_id={"epoch": ahead}, device_id_type=MESH)

    def send_all(src, dst, which):
        def one(step, carry):
            peer = peer_at(me, step, parts)
            pltpu.make_async_remote_copy(
                src_ref=src(peer),
                dst_ref=dst.at[me],
                send_sem=send_sem.at[which],
                recv_sem=recv_sem.at[which],
                device_id={"dom": peer},
                device_id_type=MESH,
            ).start()
            return carry

        lax.fori_loop(0, parts - 1, one, 0)
        pltpu.make_async_copy(src(me), dst.at[me], recv_sem.at[which]).start()

    def wait_recv(dst, which):
        pltpu.make_async_copy(dst, dst, recv_sem.at[which]).wait()

    def wait_send(dst, which):
        sent = dst.at[pl.ds(0, parts - 1)]
        pltpu.make_async_copy(sent, sent, send_sem.at[which]).wait()

    ends = 2 * events
    o = jnp.concatenate([own[0:1, :], own[1:2, :]], axis=1)
    r = jnp.concatenate([row[0:1, :], row[1:2, :]], axis=1) + 1
    owned = iota((parts, ends), 0) == o
    owned_b = onehot(owned)
    earlier = onehot(iota((ends, ends), 0) < iota((ends, ends), 1))
    before = dot(owned_b, earlier)
    rank = jnp.sum(jnp.where(owned, before, 0.0), axis=0, keepdims=True)
    rank_i = rank.astype(jnp.int32)
    ranked = iota((LANES, ends), 0) == rank_i
    high = jnp.where(ranked, (r // 32).astype(F32), 0.0).astype(BF16)
    low = jnp.where(ranked, (r % 32).astype(F32), 0.0).astype(BF16)
    asked = dot_nt(owned_b, high) * 32.0 + dot_nt(owned_b, low)
    req_s[...] = asked.reshape(parts, 1, LANES)

    pl.semaphore_wait(barrier, parts)
    send_all(lambda peer: req_s.at[peer], req_r, 0)

    place = o * CAP + rank_i
    place_s[...] = onehot(iota((slots, ends), 0) == place)
    diagonal = iota((ends, ends), 0) == iota((ends, ends), 1)
    place_col = jnp.sum(jnp.where(diagonal, place.astype(F32), 0.0), axis=1, keepdims=True)
    place_t[...] = onehot(iota((ends, slots), 1) == place_col.astype(jnp.int32))

    keyval[...] = dot(table[...], w_keyval[...]).astype(BF16)
    query[...] = dot(table[...], w_query[...]).astype(BF16)
    block = LANES
    scale = 1.0 / jnp.sqrt(jnp.float32(hsize))
    for b in range(nodes // block):
        here = pl.ds(b * block, block)
        times = jnp.zeros((nodes, block), F32)
        for j in range(nbr.shape[0]):
            times = times + jnp.where(iota((nodes, block), 0) == nbr[j : j + 1, here], 1.0, 0.0)
        for h in range(HEADS):
            cols = pl.ds(h * hsize, hsize)
            score = dot_nt(keyval[:, cols], query[here, cols]) * scale
            score = jnp.where(times > 0, score, -1e30)
            top = jnp.max(score, axis=0, keepdims=True)
            grown = jnp.exp(score - top)
            total = jnp.sum(grown * times, axis=0, keepdims=True)
            weight = (grown / total).astype(BF16).astype(F32) * times
            main = weight.astype(BF16)
            rest = (weight - main.astype(F32)).astype(BF16)
            value = keyval[:, pl.ds(width + h * hsize, hsize)]
            attended[here, cols] = (dot_tn(main, value) + dot_tn(rest, value)).astype(BF16)
    embed[...] = (table[...].astype(F32) + dot(attended[...], w_out[...])).astype(BF16)

    wait_recv(req_r, 0)
    got = jnp.broadcast_to(req_r[...], (parts, CAP, LANES))
    mine = iota((parts, CAP, LANES), 1) == iota((parts, CAP, LANES), 2)
    wanted = jnp.sum(jnp.where(mine, got, 0.0), axis=2, keepdims=True).reshape(slots, 1)
    wanted = wanted.astype(jnp.int32)
    pick[...] = onehot(iota((slots, nodes), 1) + 1 == wanted)
    mem_s[...] = pack(dot(pick[...], table[...]))
    send_all(lambda peer: mem_s.at[peer], mem_r, 1)
    emb_s[...] = pack(dot(pick[...], embed[...]))
    send_all(lambda peer: emb_s.at[peer], emb_r, 2)

    square = iota((slots, slots), 0) == iota((slots, slots), 1)
    wanted_row = jnp.sum(jnp.where(square, wanted.astype(F32), 0.0), axis=0, keepdims=True)
    pick_t[...] = onehot(iota((nodes, slots), 0) + 1 == wanted_row.astype(jnp.int32))
    hidden[...] = dot(table[...], gru_hidden[...])
    msg_edge = dot(feat[...], w_msg_edge[...])
    pair_edge = dot(feat[...], w_pair_edge[...])

    wait_recv(mem_r, 1)
    rows_back = dot(place_t[...], unpack(mem_r[...])).astype(BF16)
    to_src = dot(rows_back[events:], w_msg_mem[...]) + msg_edge
    to_dst = dot(rows_back[:events], w_msg_mem[...]) + msg_edge
    message = jnp.concatenate([to_src, to_dst], axis=0).astype(BF16)
    msg_s[...] = pack(dot(place_s[...], message))
    send_all(lambda peer: msg_s.at[peer], msg_r, 3)

    wait_recv(emb_r, 2)
    ends_back = dot(place_t[...], unpack(emb_r[...]))
    pair = ends_back[:events] * ends_back[events:] + pair_edge
    sum_one = jnp.sum(pair, axis=0, keepdims=True)
    sum_two = jnp.sum(pair * pair, axis=0, keepdims=True)
    quarters = [
        sum_one[:, :LANES],
        sum_one[:, LANES:],
        sum_two[:, :LANES],
        sum_two[:, LANES:],
    ]
    for k, quarter in enumerate(quarters):
        st_s[k] = quarter
    copies = []
    for by in range(1, PLANE):
        copies.append(
            pltpu.make_async_remote_copy(
                src_ref=st_s,
                dst_ref=st_r.at[by - 1],
                send_sem=st_send.at[by - 1],
                recv_sem=st_recv.at[by - 1],
                device_id={"dom": plane_peer(me, by, parts)},
                device_id_type=MESH,
            )
        )
    for copy in copies:
        copy.start()
    for copy in copies:
        copy.wait()
    tot_s[...] = st_s[...] + st_r[0] + st_r[1] + st_r[2]
    rings = parts // PLANE
    spot = (me // (rings * CORES)) * CORES + me % CORES
    send_all(lambda peer: tot_s.at[spot], tot_r, 4)

    wait_recv(msg_r, 3)
    inbox = unpack(msg_r[...])
    chunk = nodes // NODE_CHUNKS
    hands = []
    for c in range(NODE_CHUNKS):
        here = pl.ds(c * chunk, chunk)
        picked = pick_t[here, :]
        count = jnp.sum(picked.astype(F32), axis=1, keepdims=True)
        avg = (dot(picked, inbox) / jnp.maximum(count, 1.0)).astype(BF16)
        inp = dot(avg, gru_input[...]) + gru_bias[...]
        hid = hidden[here, :]
        reset = jax.nn.sigmoid(inp[:, :width] + hid[:, :width])
        update = jax.nn.sigmoid(inp[:, width : 2 * width] + hid[:, width : 2 * width])
        cand = jnp.tanh(inp[:, 2 * width :] + reset * hid[:, 2 * width :])
        fresh = (1.0 - update) * cand + update * table[here, :].astype(F32)
        hand_s[here, :] = jnp.where(count > 0, fresh, UNTOUCHED).astype(BF16)
        hand = pltpu.make_async_remote_copy(
            src_ref=hand_s.at[here],
            dst_ref=hand_r.at[here],
            send_sem=hand_send.at[c],
            recv_sem=hand_recv.at[c],
            device_id={"epoch": after},
            device_id_type=MESH,
        )
        hand.start()
        hands.append(hand)

    wait_recv(tot_r, 4)
    sums = [jnp.zeros((1, LANES), F32) for _ in range(PLANE)]
    for k in range(PLANE):
        for z in range(rings):
            sums[k] = sums[k] + tot_r[(k // CORES) * rings * CORES + z * CORES + k % CORES]
    count_all = jnp.float32(events * parts)
    mean = jnp.concatenate([sums[0], sums[1]], axis=1) / count_all
    var = jnp.concatenate([sums[2], sums[3]], axis=1) / count_all - mean * mean
    normed = (pair - mean) * lax.rsqrt(var + 1e-05) * bn_gain[...] + bn_shift[...]
    weighed = jnp.maximum(normed, 0.0) * w_score[...].astype(F32)
    logit_col = jnp.sum(weighed, axis=1, keepdims=True)
    corner = iota((events, events), 0) == iota((events, events), 1)
    logit = jnp.sum(jnp.where(corner, logit_col, 0.0), axis=0, keepdims=True)
    soft = jnp.maximum(logit, 0.0) + jnp.log1p(jnp.exp(-jnp.abs(logit)))
    terms = soft - lab[...].astype(F32) * logit
    ls_s[...] = jnp.broadcast_to(jnp.sum(terms, axis=1, keepdims=True), (1, LANES))
    send_all(lambda peer: ls_s, ls_r, 5)

    for c in range(NODE_CHUNKS):
        here = pl.ds(c * chunk, chunk)
        hands[c].wait()
        handed = hand_r[here, :].astype(F32)
        fresh = hand_s[here, :].astype(F32)
        old = table[here, :].astype(F32)
        prior = jnp.where(jnp.logical_and(handed < UNTOUCHED / 2, group > 0), handed, old)
        out[here, :] = jnp.where(fresh < UNTOUCHED / 2, fresh, prior).astype(BF16)

    wait_recv(ls_r, 5)
    loss[...] = jnp.sum(ls_r[...], axis=0) / count_all

    wait_send(req_s, 0)
    wait_send(mem_s, 1)
    wait_send(emb_s, 2)
    wait_send(msg_s, 3)
    wait_send(tot_r, 4)
    wait_send(ls_r, 5)


def shards(
    parts,
    groups,
    memory,
    neighbours,
    owners,
    rows,
    edge_feat,
    labels,
    w_query,
    w_keyval,
    w_out,
    w_msg_mem,
    w_msg_edge,
    w_pair_edge,
    gru_input,
    gru_hidden,
    gru_bias,
    bn_gain,
    bn_shift,
    w_score,
):
    nodes, width = memory.shape[1:]
    events = owners.shape[1]
    slots = parts * CAP
    ends = 2 * events
    block = (parts, 2 * CAP, LANES)
    line = (parts, 1, LANES)
    result, loss = pl.pallas_call(
        functools.partial(kernel, parts, groups),
        out_shape=(
            jax.ShapeDtypeStruct((nodes, width), BF16),
            jax.ShapeDtypeStruct((1, LANES), F32),
        ),
        in_specs=[pl.BlockSpec(memory_space=pltpu.VMEM)] * 18,
        out_specs=(pl.BlockSpec(memory_space=pltpu.VMEM),) * 2,
        scratch_shapes=[
            pltpu.VMEM(line, F32),
            pltpu.VMEM(line, F32),
            pltpu.VMEM(block, BF16),
            pltpu.VMEM(block, BF16),
            pltpu.VMEM(block, BF16),
            pltpu.VMEM(block, BF16),
            pltpu.VMEM(block, BF16),
            pltpu.VMEM(block, BF16),
            pltpu.VMEM((PLANE, 1, LANES), F32),
            pltpu.VMEM((PLANE - 1, PLANE, 1, LANES), F32),
            pltpu.VMEM((PLANE, 1, LANES), F32),
            pltpu.VMEM(line, F32),
            pltpu.VMEM((1, LANES), F32),
            pltpu.VMEM(line, F32),
            pltpu.VMEM((nodes, width), BF16),
            pltpu.VMEM((nodes, width), BF16),
            pltpu.VMEM((nodes, 2 * width), BF16),
            pltpu.VMEM((nodes, width), BF16),
            pltpu.VMEM((nodes, width), BF16),
            pltpu.VMEM((nodes, width), BF16),
            pltpu.VMEM((nodes, 3 * width), F32),
            pltpu.VMEM((slots, nodes), BF16),
            pltpu.VMEM((nodes, slots), BF16),
            pltpu.VMEM((slots, ends), BF16),
            pltpu.VMEM((ends, slots), BF16),
            pltpu.SemaphoreType.DMA((6,)),
            pltpu.SemaphoreType.DMA((6,)),
            pltpu.SemaphoreType.DMA((PLANE - 1,)),
            pltpu.SemaphoreType.DMA((PLANE - 1,)),
            pltpu.SemaphoreType.DMA((NODE_CHUNKS,)),
            pltpu.SemaphoreType.DMA((NODE_CHUNKS,)),
        ],
        compiler_params=pltpu.CompilerParams(
            collective_id=0, has_side_effects=True, vmem_limit_bytes=48 * 1024 * 1024
        ),
        name="window",
    )(
        memory[0],
        neighbours.T,
        owners[0].T,
        rows[0].T,
        edge_feat[0],
        labels,
        w_query,
        w_keyval,
        w_out,
        w_msg_mem,
        w_msg_edge,
        w_pair_edge,
        gru_input,
        gru_hidden,
        gru_bias[None],
        bn_gain[None],
        bn_shift[None],
        w_score[None],
    )
    return result[None], loss[0, :1]


def solution(mesh):
    parts, groups = mesh.shape["dom"], mesh.shape["epoch"]
    return jax.shard_map(
        functools.partial(shards, parts, groups),
        mesh=mesh,
        in_specs=(
            P("epoch", "dom", None),
            P("dom", None),
            P("epoch", "dom", None),
            P("epoch", "dom", None),
            P("epoch", "dom", None),
            P("epoch", "dom"),
            P(),
            P(),
            P(),
            P(),
            P(),
            P(),
            P(),
            P(),
            P(),
            P(),
            P(),
            P(),
        ),
        out_specs=(P("epoch", "dom", None), P("epoch")),
        check_vma=False,
    )
```

time: 455 us -> 89.7 us (0.20)
  blocking collectives: 264 us -> 0 us
  Pallas kernels: 0 us -> 75.4 us
  local copies, waits for them, and re-layouts: 75.5 us -> 11.9 us
  starting transfers between devices: 42.3 us -> 0 us
  waiting for transfers between devices: 37.1 us -> 0 us
  other arithmetic: 17.6 us -> 0 us
  matrix products: 14.8 us -> 0 us
    psum x2 -> x0, blocking collectives: 264 us -> none  [the longest x1 134 us: shards(): loss = lax.psum(jnp.sum(terms), 'dom') / total]
    pallas_call x0 -> x1, Pallas kernels: none -> 75.4 us  [shards(): pl.pallas_call(functools.partial(kernel, parts, groups), out_shape=(jax.S...]
    gather x9 -> x0, local copies, waits for them, and re-layouts: 45.4 us -> none  [the longest x3 32.9 us: shards(): gathered = keyval[neighbours[safe]]]
    all_to_all x4 -> x0, waiting for transfers between devices: 37.1 us -> none  [the longest x1 17.8 us: shards(): lax.all_to_all(mrow, 'dom', split_axis=0, concat_axis=0, tiled=True)]
    all_to_all x4 -> x0, starting transfers between devices: 36.9 us -> none  [the longest x1 19.8 us: shards(): lax.all_to_all(request, 'dom', split_axis=0, concat_axis=0, tiled=True)]
    dot_general x11 -> x0, matrix products: 14.8 us -> none  [the longest x1 3.07 us: shards(): jnp.einsum('abhj,abjhd->abhd', probs, values, preferred_element_type=jnp....]
    reshape x6 -> x0, local copies, waits for them, and re-layouts: 10.6 us -> none  [the longest x1 10.3 us: shards(): values = gathered[..., width:].reshape(src, cnt, -1, heads, hsize)]
    unnamed x45 -> x37, local copies, waits for them, and re-layouts: 3.22 us -> 11.9 us
  transfers between devices with their start and end apart: 6 -> 0, of which waited for: 3 -> 0; matrix products, arithmetic and copies ran while one was open for 10% -> 0% of each run, Pallas kernels for 0% -> 0%
where the time goes in v1:
time: 89.7 us; the launch traced here: 89.1 us
  Pallas kernels  75.4 us (84%)
  local copies, waits for them, and re-layouts  11.9 us (13%)
  between operations  1.87 us (2%)
    pallas_call x1, Pallas kernels, shards(): pl.pallas_call(functools.partial(kernel, parts, groups), out_shape=(jax.S...  75.4 us
    unnamed x37, local copies, waits for them, and re-layouts  11.9 us

profile of v1, /device:TPU:1, one launch (start us, length us, event | category | flops | bytes accessed | tf_op | source)
XLA Modules:
  0.0 89.1 jit_solution(2926894622174586445)
XLA Ops:
  0.6 0.0 copy-start.16
  0.6 0.0 copy-start.17
  0.6 0.7 copy-done.17
  1.3 0.0 copy-done.16
  1.3 0.0 copy-start.11
  1.3 0.0 copy-start.12
  1.3 0.0 copy-start.13
  1.3 0.0 copy-start.14
  1.3 0.0 copy-start.15
  1.4 0.6 copy-done.11
  2.0 0.0 copy-done.12
  2.0 0.0 copy-done.13
  2.0 0.0 copy-done.14
  2.0 0.0 copy-done.15
  2.0 0.0 copy-start
  2.0 1.0 %copy-done = bf16[256,768]{1,0:T(8,128)(2,1)S(1)} copy-done((bf16[256,768]{1,0:T(8,128)(2,1)S(1)}, bf16[256,768]{1,0:T(8,128)(2,1)}, u32[]{:S(2)}) %copy-start) | copy-done | bytes 393240
  3.0 0.0 copy-start.1
  3.0 1.0 %copy-done.1 = bf16[256,768]{1,0:T(8,128)(2,1)S(1)} copy-done((bf16[256,768]{1,0:T(8,128)(2,1)S(1)}, bf16[256,768]{1,0:T(8,128)(2,1)}, u32[]{:S(2)}) %copy-start.1) | copy-done | bytes 393240
  4.0 0.0 copy-start.2
  4.0 0.9 %copy-done.2 = bf16[1,512,256]{2,1,0:T(8,128)(2,1)S(1)} copy-done((bf16[1,512,256]{2,1,0:T(8,128)(2,1)S(1)}, bf16[1,512,256]{2,1,0:T(8,128)(2,1)}, u32[]{:S(2)}) %copy-start.2) | copy-done | bytes 262168
  5.0 0.0 copy-start.3
  5.0 0.9 %copy-done.3 = bf16[256,512]{1,0:T(8,128)(2,1)S(1)} copy-done((bf16[256,512]{1,0:T(8,128)(2,1)S(1)}, bf16[256,512]{1,0:T(8,128)(2,1)}, u32[]{:S(2)}) %copy-start.3) | copy-done | bytes 262168
  5.9 0.0 copy-start.4
  5.9 0.9 %copy-done.4 = bf16[256,256]{1,0:T(8,128)(2,1)S(1)} copy-done((bf16[256,256]{1,0:T(8,128)(2,1)S(1)}, bf16[256,256]{1,0:T(8,128)(2,1)}, u32[]{:S(2)}) %copy-start.4) | copy-done | bytes 131096
  6.8 0.0 copy-start.5
  6.8 0.9 %copy-done.5 = bf16[256,256]{1,0:T(8,128)(2,1)S(1)} copy-done((bf16[256,256]{1,0:T(8,128)(2,1)S(1)}, bf16[256,256]{1,0:T(8,128)(2,1)}, u32[]{:S(2)}) %copy-start.5) | copy-done | bytes 131096
  7.8 0.0 copy-start.6
  7.8 0.9 %copy-done.6 = bf16[256,256]{1,0:T(8,128)(2,1)S(1)} copy-done((bf16[256,256]{1,0:T(8,128)(2,1)S(1)}, bf16[256,256]{1,0:T(8,128)(2,1)}, u32[]{:S(2)}) %copy-start.6) | copy-done | bytes 131096
  8.7 0.0 copy-start.7
  8.7 0.8 copy-done.7
  9.5 0.0 copy-start.8
  9.5 0.8 copy-done.8
  10.3 0.0 copy-start.9
  10.3 0.8 copy-done.9
  11.1 0.0 copy-start.10
  11.1 0.8 copy-done.10
  11.9 75.4 %window.1 = (bf16[512,256]{1,0:T(8,128)(2,1)S(1)}, f32[1,128]{1,0:T(1,128)S(1)}) custom-call(bf16[512,256]{1,0:T(8,128)(2,1)S(1)} %bitcast.15, s32[10,512]{1,0:T(8,128)S(1)} %bitcast.16, s32[2,128]{1,0:T(2,128)S(1)} %bitcast.18, s32[2,128]{1,0:T(2,128)S(1)} %bitcast.19, bf16[128,128]{1,0:T(8,128)(2,1)S(1)} %bitcast.17, s32[1,128]{1,0:T(1,128)S(1)} %copy-done.15, ...), custom_call_target="tpu_custom_call" | custom-call | tf_op jit(solution)/shard_map/window/pallas_call | solution.py:376
  87.3 0.7 copy.22
  (2 shorter events, 0.0 us)
Async XLA Ops:
  0.6 0.7 copy-start.16
  0.6 0.7 copy-start.17
  1.3 0.7 copy-start.11
  1.3 0.7 copy-start.12
  1.3 0.7 copy-start.13
  1.3 0.7 copy-start.14
  1.3 0.7 copy-start.15
  2.0 1.0 %copy-start = (bf16[256,768]{1,0:T(8,128)(2,1)S(1)}, bf16[256,768]{1,0:T(8,128)(2,1)}, u32[]{:S(2)}) copy-start(bf16[256,768]{1,0:T(8,128)(2,1)} %gru_input.1) | copy-start | bytes 1179652
  3.0 1.0 %copy-start.1 = (bf16[256,768]{1,0:T(8,128)(2,1)S(1)}, bf16[256,768]{1,0:T(8,128)(2,1)}, u32[]{:S(2)}) copy-start(bf16[256,768]{1,0:T(8,128)(2,1)} %gru_hidden.1) | copy-start | bytes 1179652
  4.0 0.9 %copy-start.2 = (bf16[1,512,256]{2,1,0:T(8,128)(2,1)S(1)}, bf16[1,512,256]{2,1,0:T(8,128)(2,1)}, u32[]{:S(2)}) copy-start(bf16[1,512,256]{2,1,0:T(8,128)(2,1)} %param.18) | copy-start | bytes 786436
  5.0 0.9 %copy-start.3 = (bf16[256,512]{1,0:T(8,128)(2,1)S(1)}, bf16[256,512]{1,0:T(8,128)(2,1)}, u32[]{:S(2)}) copy-start(bf16[256,512]{1,0:T(8,128)(2,1)} %w_keyval.1) | copy-start | bytes 786436
  5.9 0.9 %copy-start.4 = (bf16[256,256]{1,0:T(8,128)(2,1)S(1)}, bf16[256,256]{1,0:T(8,128)(2,1)}, u32[]{:S(2)}) copy-start(bf16[256,256]{1,0:T(8,128)(2,1)} %w_query.1) | copy-start | bytes 393220
  6.8 0.9 %copy-start.5 = (bf16[256,256]{1,0:T(8,128)(2,1)S(1)}, bf16[256,256]{1,0:T(8,128)(2,1)}, u32[]{:S(2)}) copy-start(bf16[256,256]{1,0:T(8,128)(2,1)} %w_out.1) | copy-start | bytes 393220
  7.8 0.9 %copy-start.6 = (bf16[256,256]{1,0:T(8,128)(2,1)S(1)}, bf16[256,256]{1,0:T(8,128)(2,1)}, u32[]{:S(2)}) copy-start(bf16[256,256]{1,0:T(8,128)(2,1)} %w_msg_mem.1) | copy-start | bytes 393220
  8.7 0.8 copy-start.7
  9.5 0.8 copy-start.8
  10.3 0.8 copy-start.9
  11.1 0.8 copy-start.10

commit v2 on v1

v2 whole, which is shorter than its diff:
```python
import functools

import jax
import jax.numpy as jnp
from jax import lax
from jax.experimental import pallas as pl
from jax.experimental.pallas import tpu as pltpu
from jax.sharding import PartitionSpec as P

MESH = pl.DeviceIdType.MESH
F32 = jnp.float32
BF16 = jnp.bfloat16
VMEM_LIMIT = 62 * 1024 * 1024
CAP = 8
HEADS = 2
LANES = 128
CORES = 2
HALVES = 2
PLANE = CORES * HALVES
UNTOUCHED = 1e30
NODE_CHUNKS = 4
ORDER_M = (3, 2, 0, 1)
ORDER_E = (0, 1, 2, 3)
GROUPS = 4
TURNS = 4
EARLY = 3
LOAD_ORDER = (2, 3, 0, 7, 1, 6, 8, 4, 10, 9, 11, 13, 12, 14, 15, 16, 17, 5)


def iota(shape, dim):
    return lax.broadcasted_iota(jnp.int32, shape, dim)


def dot(a, b):
    return jnp.dot(a, b, preferred_element_type=F32)


def dot_nt(a, b):
    return lax.dot_general(a, b, (((1,), (1,)), ((), ())), preferred_element_type=F32)


def dot_tn(a, b):
    return lax.dot_general(a, b, (((0,), (0,)), ((), ())), preferred_element_type=F32)


def onehot(mask):
    return jnp.where(mask, 1.0, 0.0).astype(BF16)


def pack(x):
    rows = x.shape[0] // CAP
    left = x[:, :LANES].reshape(rows, CAP, LANES)
    right = x[:, LANES:].reshape(rows, CAP, LANES)
    return jnp.concatenate([left, right], axis=1).astype(BF16)


def unpack(x):
    rows = x.shape[0]
    x = x.astype(F32)
    left = x[:, :CAP].reshape(rows * CAP, LANES)
    right = x[:, CAP:].reshape(rows * CAP, LANES)
    return jnp.concatenate([left, right], axis=1).astype(BF16)


def along(turn, rings):
    half = (turn + 1) // 2
    if isinstance(turn, int):
        return rings // 2 + (half if turn % 2 else rings - half)
    return rings // 2 + jnp.where(lax.rem(turn, 2) == 1, half, rings - half)


def facing(turn, rings):
    if isinstance(turn, int):
        if turn in (0, rings - 1):
            return turn
        return turn + 1 if turn % 2 else turn - 1
    return turn + jnp.where(lax.rem(turn, 2) == 1, 1, -1)


def kernel(
    parts,
    groups,
    table_h,
    nbr_h,
    own_h,
    row_h,
    feat_h,
    lab_h,
    w_query_h,
    w_keyval_h,
    w_out_h,
    w_msg_mem_h,
    w_msg_edge_h,
    w_pair_edge_h,
    gru_input_h,
    gru_hidden_h,
    gru_bias_h,
    bn_gain_h,
    bn_shift_h,
    w_score_h,
    out,
    loss,
    req_s,
    req_r,
    mem_s,
    mem_r,
    emb_s,
    emb_r,
    msg_s,
    msg_r,
    st_r,
    tot_r,
    ls_r,
    hand_s,
    hand_r,
    keyval,
    query,
    attended,
    embed,
    hidden,
    pick,
    pick_t,
    place_s,
    place_t,
    times_named,
    agg,
    send_sem,
    recv_sem,
    tot_sem,
    ls_sem,
    st_send,
    st_recv,
    hand_send,
    hand_recv,
    load_sem,
    table,
    nbr,
    own,
    row,
    feat,
    lab,
    w_query,
    w_keyval,
    w_out,
    w_msg_mem,
    w_msg_edge,
    w_pair_edge,
    gru_input,
    gru_hidden,
    gru_bias,
    bn_gain,
    bn_shift,
    w_score,
):
    me = lax.axis_index("dom")
    group = lax.axis_index("epoch")
    after = lax.rem(group + 1, groups)
    ahead = lax.rem(group + groups - 1, groups)
    nodes, width = table.shape
    events = feat.shape[0]
    slots = parts * CAP
    hsize = width // HEADS
    rings = parts // PLANE
    layer = rings * CORES
    y, inner = lax.div(me, layer), lax.rem(me, layer)
    z, core = lax.div(inner, CORES), lax.rem(inner, CORES)
    spot = y * CORES + core
    offsets = []
    for by in range(PLANE):
        there = lax.rem(spot + by, PLANE)
        offsets.append(lax.div(there, CORES) * layer + lax.rem(there, CORES))

    held = (
        table,
        nbr,
        own,
        row,
        feat,
        lab,
        w_query,
        w_keyval,
        w_out,
        w_msg_mem,
        w_msg_edge,
        w_pair_edge,
        gru_input,
        gru_hidden,
        gru_bias,
        bn_gain,
        bn_shift,
        w_score,
    )
    given = (
        table_h,
        nbr_h,
        own_h,
        row_h,
        feat_h,
        lab_h,
        w_query_h,
        w_keyval_h,
        w_out_h,
        w_msg_mem_h,
        w_msg_edge_h,
        w_pair_edge_h,
        gru_input_h,
        gru_hidden_h,
        gru_bias_h,
        bn_gain_h,
        bn_shift_h,
        w_score_h,
    )
    loads = [
        pltpu.make_async_copy(src, dst, load_sem.at[k])
        for k, (src, dst) in enumerate(zip(given, held))
    ]
    for k in LOAD_ORDER:
        loads[k].start()

    barrier = pltpu.get_barrier_semaphore()

    def each_turn(visit, first, last):
        if first == 0:
            visit(0)
        top = min(last, rings - 1)

        def one(turn, carry):
            visit(turn)
            return carry

        lax.fori_loop(max(first, 1), top, one, 0)
        if last == rings:
            visit(rings - 1)

    def each_peer(turn):
        base = lax.rem(z + along(turn, rings), rings) * CORES
        own_turn = isinstance(turn, int) and turn == rings - 1
        return [(by, base + offsets[by]) for by in range(1 if own_turn else 0, PLANE)]

    def greet(turn):
        for _, peer in each_peer(turn):
            pl.semaphore_signal(barrier, inc=1, device_id={"dom": peer}, device_id_type=MESH)

    each_turn(greet, 0, rings)
    pl.semaphore_signal(barrier, inc=1, device_id={"epoch": ahead}, device_id_type=MESH)

    def remote(src, dst, sent, received, peer):
        return pltpu.make_async_remote_copy(
            src_ref=src,
            dst_ref=dst,
            send_sem=sent,
            recv_sem=received,
            device_id={"dom": peer},
            device_id_type=MESH,
        )

    def send_turns(src, dst, which, first, last):
        def visit(turn):
            back = facing(turn, rings)
            for by, peer in each_peer(turn):
                remote(
                    src.at[turn * PLANE + by],
                    dst.at[back * PLANE + (PLANE - by) % PLANE],
                    send_sem.at[which],
                    recv_sem.at[which, lax.div(back, TURNS)],
                    peer,
                ).start()

        each_turn(visit, first, last)
        if last == rings:
            here = (rings - 1) * PLANE
            pltpu.make_async_copy(
                src.at[here], dst.at[here], recv_sem.at[which, GROUPS - 1]
            ).start()

    def send_groups(src, dst, which, first, last):
        send_turns(src, dst, which, first * TURNS, last * TURNS)

    def wait_group(dst, which, g):
        block = dst.at[pl.ds(g * TURNS * PLANE, TURNS * PLANE)]
        pltpu.make_async_copy(block, block, recv_sem.at[which, g]).wait()

    def wait_sent(dst, which):
        sent = dst.at[pl.ds(0, parts - 1)]
        pltpu.make_async_copy(sent, sent, send_sem.at[which]).wait()

    loads[2].wait()
    loads[3].wait()
    ends = 2 * events
    o = jnp.concatenate([own[0:1, :], own[1:2, :]], axis=1)
    r = jnp.concatenate([row[0:1, :], row[1:2, :]], axis=1) + 1
    away = (o // CORES - z + parts) % rings
    away = jnp.where(away == 0, rings // 2, away - rings // 2)
    turn_of = jnp.where(away > 0, 2 * away - 1, -2 * away)
    o = turn_of * PLANE + (o // layer * CORES + o % CORES - spot + PLANE) % PLANE
    owned = iota((parts, ends), 0) == o
    owned_b = onehot(owned)
    earlier = onehot(iota((ends, ends), 0) < iota((ends, ends), 1))
    before = dot(owned_b, earlier)
    rank = jnp.sum(jnp.where(owned, before, 0.0), axis=0, keepdims=True)
    rank_i = rank.astype(jnp.int32)
    ranked = iota((LANES, ends), 0) == rank_i
    high = jnp.where(ranked, (r // 32).astype(F32), 0.0).astype(BF16)
    low = jnp.where(ranked, (r % 32).astype(F32), 0.0).astype(BF16)
    asked = dot_nt(owned_b, high) * 32.0 + dot_nt(owned_b, low)
    req_s[...] = asked.reshape(parts, 1, LANES)

    pl.semaphore_wait(barrier, parts)
    send_groups(req_s, req_r, 0, 0, GROUPS)

    place = o * CAP + rank_i
    place_s[...] = onehot(iota((slots, ends), 0) == place)
    diagonal = iota((ends, ends), 0) == iota((ends, ends), 1)
    place_col = jnp.sum(jnp.where(diagonal, place.astype(F32), 0.0), axis=1, keepdims=True)
    place_t[...] = onehot(iota((ends, slots), 1) == place_col.astype(jnp.int32))

    for k in (0, 1, 6, 7, 8):
        loads[k].wait()
    keyval[...] = dot(table[...], w_keyval[...]).astype(BF16)
    query[...] = dot(table[...], w_query[...]).astype(BF16)
    block = LANES
    scale = 1.0 / jnp.sqrt(jnp.float32(hsize))
    for b in range(nodes // block):
        here = pl.ds(b * block, block)
        times = jnp.zeros((nodes, block), F32)
        for j in range(nbr.shape[0]):
            times = times + jnp.where(iota((nodes, block), 0) == nbr[j : j + 1, here], 1.0, 0.0)
        for h in range(HEADS):
            cols = pl.ds(h * hsize, hsize)
            score = dot_nt(keyval[:, cols], query[here, cols]) * scale
            score = jnp.where(times > 0, score, -1e30)
            top = jnp.max(score, axis=0, keepdims=True)
            grown = jnp.exp(score - top)
            total = jnp.sum(grown * times, axis=0, keepdims=True)
            weight = (grown / total).astype(BF16).astype(F32) * times
            main = weight.astype(BF16)
            rest = (weight - main.astype(F32)).astype(BF16)
            value = keyval[:, pl.ds(width + h * hsize, hsize)]
            attended[here, cols] = (dot_tn(main, value) + dot_tn(rest, value)).astype(BF16)
    embed[...] = (table[...].astype(F32) + dot(attended[...], w_out[...])).astype(BF16)

    gslots = slots // GROUPS
    gblocks = parts // GROUPS
    mine = iota((gblocks, CAP, LANES), 1) == iota((gblocks, CAP, LANES), 2)
    asked_for = {}
    for g in ORDER_M:
        here, blocks = pl.ds(g * gslots, gslots), pl.ds(g * gblocks, gblocks)
        wait_group(req_r, 0, g)
        got = jnp.broadcast_to(req_r[blocks], (gblocks, CAP, LANES))
        wanted = jnp.sum(jnp.where(mine, got, 0.0), axis=2, keepdims=True).reshape(gslots, 1)
        asked_for[g] = wanted
        pick[here, :] = onehot(iota((gslots, nodes), 1) + 1 == wanted.astype(jnp.int32))
        mem_s[blocks] = pack(dot(pick[here, :], table[...]))
        send_groups(mem_s, mem_r, 1, g, g + 1)
    for g in ORDER_E:
        here, blocks = pl.ds(g * gslots, gslots), pl.ds(g * gblocks, gblocks)
        emb_s[blocks] = pack(dot(pick[here, :], embed[...]))
        send_groups(emb_s, emb_r, 2, g, g + 1)

    for k in (4, 5, 9, 10, 11, 12, 13, 14, 15, 16, 17):
        loads[k].wait()
    wanted = jnp.concatenate([asked_for[g] for g in range(GROUPS)], axis=0)
    square = iota((slots, slots), 0) == iota((slots, slots), 1)
    wanted_row = jnp.sum(jnp.where(square, wanted, 0.0), axis=0, keepdims=True)
    pick_t[...] = onehot(iota((nodes, slots), 0) + 1 == wanted_row.astype(jnp.int32))
    times_named[...] = dot(pick_t[...], jnp.ones((slots, LANES), BF16))
    hidden[...] = dot(table[...], gru_hidden[...])
    msg_edge = dot(feat[...], w_msg_edge[...])
    pair_edge = dot(feat[...], w_pair_edge[...])

    rows_back = jnp.zeros((ends, width), F32)
    for g in range(GROUPS):
        wait_group(mem_r, 1, g)
        blocks = pl.ds(g * gblocks, gblocks)
        rows_back = rows_back + dot(
            place_t[:, pl.ds(g * gslots, gslots)], unpack(mem_r[blocks])
        )
    rows_back = rows_back.astype(BF16)
    to_src = dot(rows_back[events:], w_msg_mem[...]) + msg_edge
    to_dst = dot(rows_back[:events], w_msg_mem[...]) + msg_edge
    message = jnp.concatenate([to_src, to_dst], axis=0).astype(BF16)
    for g in range(GROUPS):
        blocks = pl.ds(g * gblocks, gblocks)
        msg_s[blocks] = pack(dot(place_s[pl.ds(g * gslots, gslots), :], message))
        if g < EARLY:
            send_groups(msg_s, msg_r, 3, g, g + 1)

    ends_back = jnp.zeros((ends, width), F32)
    for g in range(GROUPS):
        wait_group(emb_r, 2, g)
        blocks = pl.ds(g * gblocks, gblocks)
        ends_back = ends_back + dot(
            place_t[:, pl.ds(g * gslots, gslots)], unpack(emb_r[blocks])
        )
    pair = ends_back[:events] * ends_back[events:] + pair_edge
    sum_one = jnp.sum(pair, axis=0, keepdims=True)
    sum_two = jnp.sum(pair * pair, axis=0, keepdims=True)
    st_r[pl.ds(spot, 1)] = jnp.concatenate([sum_one, sum_two], axis=1).reshape(1, 1, 2 * width)
    copies = []
    for by in range(1, PLANE):
        copies.append(
            remote(
                st_r.at[spot],
                st_r.at[spot],
                st_send.at[by - 1],
                st_recv.at[PLANE - 1 - by],
                z * CORES + offsets[by],
            )
        )
    for copy in copies:
        copy.start()
    for by in range(1, PLANE):
        other = lax.rem(spot + by, PLANE)
        remote(
            st_r.at[other], st_r.at[other], st_send.at[by - 1], st_recv.at[by - 1], me
        ).wait_recv()
    plane_sum = st_r[0:1] + st_r[1:2] + st_r[2:3] + st_r[3:4]
    tot_r[pl.ds(z, 1)] = plane_sum

    def spread_sums(step, carry):
        peer = lax.rem(z + step, rings) * CORES + offsets[0]
        remote(tot_r.at[z], tot_r.at[z], send_sem.at[4], tot_sem, peer).start()
        return carry

    lax.fori_loop(1, rings, spread_sums, 0)
    if EARLY < GROUPS:
        send_groups(msg_s, msg_r, 3, EARLY, GROUPS)

    others = tot_r.at[pl.ds(0, rings - 1)]
    pltpu.make_async_copy(others, others, tot_sem).wait()
    sums = tot_r[0]
    for k in range(1, rings):
        sums = sums + tot_r[k]
    count_all = jnp.float32(events * parts)
    mean = sums[:, :width] / count_all
    var = sums[:, width:] / count_all - mean * mean
    normed = (pair - mean) * lax.rsqrt(var + 1e-05) * bn_gain[...] + bn_shift[...]
    weighed = jnp.maximum(normed, 0.0) * w_score[...].astype(F32).reshape(1, width)
    logit_col = jnp.sum(weighed, axis=1, keepdims=True)
    corner = iota((events, events), 0) == iota((events, events), 1)
    logit = jnp.sum(jnp.where(corner, logit_col, 0.0), axis=0, keepdims=True)
    soft = jnp.maximum(logit, 0.0) + jnp.log1p(jnp.exp(-jnp.abs(logit)))
    terms = soft - lab[...].astype(F32) * logit
    part = jnp.sum(terms, axis=1, keepdims=True)
    ls_r[pl.ds(me, 1)] = jnp.broadcast_to(part, (1, LANES)).reshape(1, 1, LANES)

    def spread_loss(turn):
        for _, peer in each_peer(turn):
            remote(ls_r.at[me], ls_r.at[me], send_sem.at[5], ls_sem, peer).start()

    each_turn(spread_loss, 0, rings)

    chunk = nodes // NODE_CHUNKS
    for g in range(GROUPS - 1):
        wait_group(msg_r, 3, g)
        blocks = pl.ds(g * gblocks, gblocks)
        part = dot(pick_t[:, pl.ds(g * gslots, gslots)], unpack(msg_r[blocks]))
        agg[...] = part if g == 0 else agg[...] + part
    wait_group(msg_r, 3, GROUPS - 1)
    inbox = unpack(msg_r[pl.ds(parts - gblocks, gblocks)])
    hands = []
    for c in range(NODE_CHUNKS):
        here = pl.ds(c * chunk, chunk)
        count = jnp.concatenate([times_named[here, :], times_named[here, :]], axis=1)
        total = agg[here, :] + dot(pick_t[here, pl.ds(slots - gslots, gslots)], inbox)
        avg = (total / jnp.maximum(count, 1.0)).astype(BF16)
        inp = dot(avg, gru_input[...]) + gru_bias[...].reshape(1, 3 * width)
        hid = hidden[here, :]
        reset = jax.nn.sigmoid(inp[:, :width] + hid[:, :width])
        update = jax.nn.sigmoid(inp[:, width : 2 * width] + hid[:, width : 2 * width])
        cand = jnp.tanh(inp[:, 2 * width :] + reset * hid[:, 2 * width :])
        fresh = (1.0 - update) * cand + update * table[here, :].astype(F32)
        hand_s[here, :] = jnp.where(count > 0, fresh, UNTOUCHED).astype(BF16)
        hand = pltpu.make_async_remote_copy(
            src_ref=hand_s.at[here],
            dst_ref=hand_r.at[here],
            send_sem=hand_send.at[c],
            recv_sem=hand_recv.at[c],
            device_id={"epoch": after},
            device_id_type=MESH,
        )
        hand.start()
        hands.append(hand)

    for c in range(NODE_CHUNKS):
        here = pl.ds(c * chunk, chunk)
        hands[c].wait()
        handed = hand_r[here, :].astype(F32)
        fresh = hand_s[here, :].astype(F32)
        old = table[here, :].astype(F32)
        prior = jnp.where(jnp.logical_and(handed < UNTOUCHED / 2, group > 0), handed, old)
        out[here, :] = jnp.where(fresh < UNTOUCHED / 2, fresh, prior).astype(BF16)

    others = ls_r.at[pl.ds(0, parts - 1)]
    pltpu.make_async_copy(others, others, ls_sem).wait()
    loss[...] = jnp.sum(ls_r[...], axis=0) / count_all

    wait_sent(req_s, 0)
    wait_sent(mem_s, 1)
    wait_sent(emb_s, 2)
    wait_sent(msg_s, 3)
    for copy in copies:
        copy.wait_send()
    others = tot_r.at[pl.ds(0, rings - 1)]
    pltpu.make_async_copy(others, others, send_sem.at[4]).wait()
    wait_sent(ls_r, 5)


def shards(
    parts,
    groups,
    memory,
    neighbours,
    owners,
    rows,
    edge_feat,
    labels,
    w_query,
    w_keyval,
    w_out,
    w_msg_mem,
    w_msg_edge,
    w_pair_edge,
    gru_input,
    gru_hidden,
    gru_bias,
    bn_gain,
    bn_shift,
    w_score,
):
    nodes, width = memory.shape[1:]
    events = owners.shape[1]
    slots = parts * CAP
    ends = 2 * events
    block = (parts, 2 * CAP, LANES)
    line = (parts, 1, LANES)
    operands = (
        memory[0],
        neighbours.T,
        owners[0].T,
        rows[0].T,
        edge_feat[0],
        labels,
        w_query,
        w_keyval,
        w_out,
        w_msg_mem,
        w_msg_edge,
        w_pair_edge,
        gru_input,
        gru_hidden,
        gru_bias,
        bn_gain[None],
        bn_shift[None],
        w_score,
    )
    result, loss = pl.pallas_call(
        functools.partial(kernel, parts, groups),
        out_shape=(
            pltpu.VMEM((nodes, width), BF16),
            pltpu.VMEM((1, LANES), F32),
        ),
        in_specs=[pl.BlockSpec(memory_space=pl.ANY)] * 18,
        out_specs=(pl.BlockSpec(memory_space=pltpu.VMEM),) * 2,
        scratch_shapes=[
            pltpu.VMEM(line, F32),
            pltpu.VMEM(line, F32),
            pltpu.VMEM(block, BF16),
            pltpu.VMEM(block, BF16),
            pltpu.VMEM(block, BF16),
            pltpu.VMEM(block, BF16),
            pltpu.VMEM(block, BF16),
            pltpu.VMEM(block, BF16),
            pltpu.VMEM((PLANE, 1, 2 * width), F32),
            pltpu.VMEM((parts // PLANE, 1, 2 * width), F32),
            pltpu.VMEM(line, F32),
            pltpu.VMEM((nodes, width), BF16),
            pltpu.VMEM((nodes, width), BF16),
            pltpu.VMEM((nodes, 2 * width), BF16),
            pltpu.VMEM((nodes, width), BF16),
            pltpu.VMEM((nodes, width), BF16),
            pltpu.VMEM((nodes, width), BF16),
            pltpu.VMEM((nodes, 3 * width), F32),
            pltpu.VMEM((slots, nodes), BF16),
            pltpu.VMEM((nodes, slots), BF16),
            pltpu.VMEM((slots, ends), BF16),
            pltpu.VMEM((ends, slots), BF16),
            pltpu.VMEM((nodes, LANES), F32),
            pltpu.VMEM((nodes, width), F32),
            pltpu.SemaphoreType.DMA((6,)),
            pltpu.SemaphoreType.DMA((4, GROUPS)),
            pltpu.SemaphoreType.DMA,
            pltpu.SemaphoreType.DMA,
            pltpu.SemaphoreType.DMA((PLANE - 1,)),
            pltpu.SemaphoreType.DMA((PLANE - 1,)),
            pltpu.SemaphoreType.DMA((NODE_CHUNKS,)),
            pltpu.SemaphoreType.DMA((NODE_CHUNKS,)),
            pltpu.SemaphoreType.DMA((len(operands),)),
        ]
        + [pltpu.VMEM(x.shape, x.dtype) for x in operands],
        compiler_params=pltpu.CompilerParams(
            collective_id=0, has_side_effects=True, vmem_limit_bytes=VMEM_LIMIT
        ),
        name="window",
    )(*operands)
    return result[None], loss[0, :1]


def solution(mesh):
    parts, groups = mesh.shape["dom"], mesh.shape["epoch"]
    return jax.shard_map(
        functools.partial(shards, parts, groups),
        mesh=mesh,
        in_specs=(
            P("epoch", "dom", None),
            P("dom", None),
            P("epoch", "dom", None),
            P("epoch", "dom", None),
            P("epoch", "dom", None),
            P("epoch", "dom"),
            P(),
            P(),
            P(),
            P(),
            P(),
            P(),
            P(),
            P(),
            P(),
            P(),
            P(),
            P(),
        ),
        out_specs=(P("epoch", "dom", None), P("epoch")),
        check_vma=False,
    )
```

time: 89.7 us -> 75.3 us (0.84)
  local copies, waits for them, and re-layouts: 11.9 us -> 0.71 us
  Pallas kernels: 75.4 us -> 72.6 us
    unnamed x37 -> x1, local copies, waits for them, and re-layouts: 11.9 us -> 0.71 us
    pallas_call x1, Pallas kernels: 75.4 us -> 72.6 us  [shards(): pl.pallas_call(functools.partial(kernel, parts, groups), out_shape=(pltpu...]
where the time goes in v2:
time: 75.3 us; the launch traced here: 75.2 us
  Pallas kernels  72.6 us (96%)
  between operations  1.81 us (2%)
    pallas_call x1, Pallas kernels, shards(): pl.pallas_call(functools.partial(kernel, parts, groups), out_shape=(pltpu...  72.6 us

profile of v2, /device:TPU:1, one launch (start us, length us, event | category | flops | bytes accessed | tf_op | source)
XLA Modules:
  0.0 75.2 jit_solution(10607483328005582675)
XLA Ops:
  0.6 72.6 %window.1 = (bf16[512,256]{1,0:T(8,128)(2,1)S(1)}, f32[1,128]{1,0:T(1,128)S(1)}) custom-call(bf16[512,256]{1,0:T(8,128)(2,1)} %bitcast.16, s32[10,512]{1,0:T(8,128)} %bitcast.17, s32[2,128]{1,0:T(2,128)} %bitcast.19, s32[2,128]{1,0:T(2,128)} %bitcast.20, bf16[128,128]{1,0:T(8,128)(2,1)} %bitcast.18, s32[1,128]{1,0:T(1,128)} %lab_h.1, ...), custom_call_target="tpu_custom_call" | custom-call | tf_op jit(solution)/shard_map/window/pallas_call | solution.py:557
  73.3 0.7 copy.22

commit v3 on v2

--- a/solution.py
+++ b/solution.py
@@ -21,6 +21,7 @@
 NODE_CHUNKS = 4
 ORDER_M = (3, 2, 0, 1)
 ORDER_E = (0, 1, 2, 3)
+NEAR = 7
 GROUPS = 4
 TURNS = 4
 EARLY = 3
@@ -75,6 +76,10 @@
             return turn
         return turn + 1 if turn % 2 else turn - 1
     return turn + jnp.where(lax.rem(turn, 2) == 1, 1, -1)
+
+
+def halfway(turn, rings):
+    return rings // 4 if turn % 2 == 0 else rings - rings // 4
 
 
 def kernel(
@@ -126,6 +131,9 @@
     agg,
     send_sem,
     recv_sem,
+    relay,
+    relay_send,
+    relay_recv,
     tot_sem,
     ls_sem,
     st_send,
@@ -214,7 +222,7 @@
         pltpu.make_async_copy(src, dst, load_sem.at[k])
         for k, (src, dst) in enumerate(zip(given, held))
     ]
-    for k in LOAD_ORDER:
+    for k in LOAD_ORDER[:2]:
         loads[k].start()
 
     barrier = pltpu.get_barrier_semaphore()
@@ -241,8 +249,10 @@
         for _, peer in each_peer(turn):
             pl.semaphore_signal(barrier, inc=1, device_id={"dom": peer}, device_id_type=MESH)
 
-    each_turn(greet, 0, rings)
+    each_turn(greet, NEAR, rings)
     pl.semaphore_signal(barrier, inc=1, device_id={"epoch": ahead}, device_id_type=MESH)
+    for k in LOAD_ORDER[2:]:
+        loads[k].start()
 
     def remote(src, dst, sent, received, peer):
         return pltpu.make_async_remote_copy(
@@ -305,8 +315,12 @@
     asked = dot_nt(owned_b, high) * 32.0 + dot_nt(owned_b, low)
     req_s[...] = asked.reshape(parts, 1, LANES)
 
-    pl.semaphore_wait(barrier, parts)
-    send_groups(req_s, req_r, 0, 0, GROUPS)
+    pl.semaphore_wait(barrier, (rings - NEAR) * PLANE)
+    for turn in range(NEAR):
+        blocks = pl.ds(turn * PLANE, PLANE)
+        peer = lax.rem(z + halfway(turn, rings), rings) * CORES + offsets[0]
+        remote(req_s.at[blocks], relay.at[blocks], relay_send, relay_recv, peer).start()
+    send_turns(req_s, req_r, 0, NEAR, rings)
 
     place = o * CAP + rank_i
     place_s[...] = onehot(iota((slots, ends), 0) == place)
@@ -318,6 +332,34 @@
         loads[k].wait()
     keyval[...] = dot(table[...], w_keyval[...]).astype(BF16)
     query[...] = dot(table[...], w_query[...]).astype(BF16)
+
+    pltpu.make_async_copy(relay, relay, relay_recv).wait()
+    for turn in range(NEAR):
+        onward = along(turn, rings) - halfway(turn, rings) + rings
+        base = lax.rem(z + onward, rings) * CORES
+        back = facing(turn, rings)
+        for by in range(PLANE):
+            remote(
+                relay.at[turn * PLANE + by],
+                req_r.at[back * PLANE + (PLANE - by) % PLANE],
+                send_sem.at[0],
+                recv_sem.at[0, back // TURNS],
+                base + offsets[by],
+            ).start()
+
+    gslots = slots // GROUPS
+    gblocks = parts // GROUPS
+    mine = iota((gblocks, CAP, LANES), 1) == iota((gblocks, CAP, LANES), 2)
+    asked_for = {}
+    for g in ORDER_M:
+        here, blocks = pl.ds(g * gslots, gslots), pl.ds(g * gblocks, gblocks)
+        wait_group(req_r, 0, g)
+        got = jnp.broadcast_to(req_r[blocks], (gblocks, CAP, LANES))
+        wanted = jnp.sum(jnp.where(mine, got, 0.0), axis=2, keepdims=True).reshape(gslots, 1)
+        asked_for[g] = wanted
+        pick[here, :] = onehot(iota((gslots, nodes), 1) + 1 == wanted.astype(jnp.int32))
+        mem_s[blocks] = pack(dot(pick[here, :], table[...]))
+        send_groups(mem_s, mem_r, 1, g, g + 1)
     block = LANES
     scale = 1.0 / jnp.sqrt(jnp.float32(hsize))
     for b in range(nodes // block):
@@ -339,19 +381,6 @@
             attended[here, cols] = (dot_tn(main, value) + dot_tn(rest, value)).astype(BF16)
     embed[...] = (table[...].astype(F32) + dot(attended[...], w_out[...])).astype(BF16)
 
-    gslots = slots // GROUPS
-    gblocks = parts // GROUPS
-    mine = iota((gblocks, CAP, LANES), 1) == iota((gblocks, CAP, LANES), 2)
-    asked_for = {}
-    for g in ORDER_M:
-        here, blocks = pl.ds(g * gslots, gslots), pl.ds(g * gblocks, gblocks)
-        wait_group(req_r, 0, g)
-        got = jnp.broadcast_to(req_r[blocks], (gblocks, CAP, LANES))
-        wanted = jnp.sum(jnp.where(mine, got, 0.0), axis=2, keepdims=True).reshape(gslots, 1)
-        asked_for[g] = wanted
-        pick[here, :] = onehot(iota((gslots, nodes), 1) + 1 == wanted.astype(jnp.int32))
-        mem_s[blocks] = pack(dot(pick[here, :], table[...]))
-        send_groups(mem_s, mem_r, 1, g, g + 1)
     for g in ORDER_E:
         here, blocks = pl.ds(g * gslots, gslots), pl.ds(g * gblocks, gblocks)
         emb_s[blocks] = pack(dot(pick[here, :], embed[...]))
@@ -426,30 +455,6 @@
     if EARLY < GROUPS:
         send_groups(msg_s, msg_r, 3, EARLY, GROUPS)
 
-    others = tot_r.at[pl.ds(0, rings - 1)]
-    pltpu.make_async_copy(others, others, tot_sem).wait()
-    sums = tot_r[0]
-    for k in range(1, rings):
-        sums = sums + tot_r[k]
-    count_all = jnp.float32(events * parts)
-    mean = sums[:, :width] / count_all
-    var = sums[:, width:] / count_all - mean * mean
-    normed = (pair - mean) * lax.rsqrt(var + 1e-05) * bn_gain[...] + bn_shift[...]
-    weighed = jnp.maximum(normed, 0.0) * w_score[...].astype(F32).reshape(1, width)
-    logit_col = jnp.sum(weighed, axis=1, keepdims=True)
-    corner = iota((events, events), 0) == iota((events, events), 1)
-    logit = jnp.sum(jnp.where(corner, logit_col, 0.0), axis=0, keepdims=True)
-    soft = jnp.maximum(logit, 0.0) + jnp.log1p(jnp.exp(-jnp.abs(logit)))
-    terms = soft - lab[...].astype(F32) * logit
-    part = jnp.sum(terms, axis=1, keepdims=True)
-    ls_r[pl.ds(me, 1)] = jnp.broadcast_to(part, (1, LANES)).reshape(1, 1, LANES)
-
-    def spread_loss(turn):
-        for _, peer in each_peer(turn):
-            remote(ls_r.at[me], ls_r.at[me], send_sem.at[5], ls_sem, peer).start()
-
-    each_turn(spread_loss, 0, rings)
-
     chunk = nodes // NODE_CHUNKS
     for g in range(GROUPS - 1):
         wait_group(msg_r, 3, g)
@@ -482,6 +487,30 @@
         hand.start()
         hands.append(hand)
 
+    others = tot_r.at[pl.ds(0, rings - 1)]
+    pltpu.make_async_copy(others, others, tot_sem).wait()
+    sums = tot_r[0]
+    for k in range(1, rings):
+        sums = sums + tot_r[k]
+    count_all = jnp.float32(events * parts)
+    mean = sums[:, :width] / count_all
+    var = sums[:, width:] / count_all - mean * mean
+    normed = (pair - mean) * lax.rsqrt(var + 1e-05) * bn_gain[...] + bn_shift[...]
+    weighed = jnp.maximum(normed, 0.0) * w_score[...].astype(F32).reshape(1, width)
+    logit_col = jnp.sum(weighed, axis=1, keepdims=True)
+    corner = iota((events, events), 0) == iota((events, events), 1)
+    logit = jnp.sum(jnp.where(corner, logit_col, 0.0), axis=0, keepdims=True)
+    soft = jnp.maximum(logit, 0.0) + jnp.log1p(jnp.exp(-jnp.abs(logit)))
+    terms = soft - lab[...].astype(F32) * logit
+    part = jnp.sum(terms, axis=1, keepdims=True)
+    ls_r[pl.ds(me, 1)] = jnp.broadcast_to(part, (1, LANES)).reshape(1, 1, LANES)
+
+    def spread_loss(turn):
+        for _, peer in each_peer(turn):
+            remote(ls_r.at[me], ls_r.at[me], send_sem.at[5], ls_sem, peer).start()
+
+    each_turn(spread_loss, 0, rings)
+
     for c in range(NODE_CHUNKS):
         here = pl.ds(c * chunk, chunk)
         hands[c].wait()
@@ -496,6 +525,7 @@
     loss[...] = jnp.sum(ls_r[...], axis=0) / count_all
 
     wait_sent(req_s, 0)
+    pltpu.make_async_copy(relay, relay, relay_send).wait()
     wait_sent(mem_s, 1)
     wait_sent(emb_s, 2)
     wait_sent(msg_s, 3)
@@ -589,6 +619,9 @@
             pltpu.VMEM((nodes, width), F32),
             pltpu.SemaphoreType.DMA((6,)),
             pltpu.SemaphoreType.DMA((4, GROUPS)),
+            pltpu.VMEM((NEAR * PLANE, 1, LANES), F32),
+            pltpu.SemaphoreType.DMA,
+            pltpu.SemaphoreType.DMA,
             pltpu.SemaphoreType.DMA,
             pltpu.SemaphoreType.DMA,
             pltpu.SemaphoreType.DMA((PLANE - 1,)),

time: 75.3 us -> 75 us (level)
  no operation moved by 1% of the time
where the time goes in v3:
time: 75 us; the launch traced here: 74.9 us
  Pallas kernels  72.3 us (96%)
  between operations  1.81 us (2%)
    pallas_call x1, Pallas kernels, shards(): pl.pallas_call(functools.partial(kernel, parts, groups), out_shape=(pltpu...  72.3 us

profile of v3, /device:TPU:1, one launch (start us, length us, event | category | flops | bytes accessed | tf_op | source)
XLA Modules:
  0.0 74.9 jit_solution(6994290370434251926)
XLA Ops:
  0.6 72.3 %window.1 = (bf16[512,256]{1,0:T(8,128)(2,1)S(1)}, f32[1,128]{1,0:T(1,128)S(1)}) custom-call(bf16[512,256]{1,0:T(8,128)(2,1)} %bitcast.16, s32[10,512]{1,0:T(8,128)} %bitcast.17, s32[2,128]{1,0:T(2,128)} %bitcast.19, s32[2,128]{1,0:T(2,128)} %bitcast.20, bf16[128,128]{1,0:T(8,128)(2,1)} %bitcast.18, s32[1,128]{1,0:T(1,128)} %lab_h.1, ...), custom_call_target="tpu_custom_call" | custom-call | tf_op jit(solution)/shard_map/window/pallas_call | solution.py:587
  73.0 0.7 copy.22

commit v4 on v3

--- a/solution.py
+++ b/solution.py
@@ -333,6 +333,25 @@
     keyval[...] = dot(table[...], w_keyval[...]).astype(BF16)
     query[...] = dot(table[...], w_query[...]).astype(BF16)
 
+    block = LANES
+    scale = 1.0 / jnp.sqrt(jnp.float32(hsize))
+    for b in range(0, 2):
+        here = pl.ds(b * block, block)
+        times = jnp.zeros((nodes, block), F32)
+        for j in range(nbr.shape[0]):
+            times = times + jnp.where(iota((nodes, block), 0) == nbr[j : j + 1, here], 1.0, 0.0)
+        for h in range(HEADS):
+            cols = pl.ds(h * hsize, hsize)
+            score = dot_nt(keyval[:, cols], query[here, cols]) * scale
+            score = jnp.where(times > 0, score, -1e30)
+            top = jnp.max(score, axis=0, keepdims=True)
+            grown = jnp.exp(score - top)
+            total = jnp.sum(grown * times, axis=0, keepdims=True)
+            weight = (grown / total).astype(BF16).astype(F32) * times
+            main = weight.astype(BF16)
+            rest = (weight - main.astype(F32)).astype(BF16)
+            value = keyval[:, pl.ds(width + h * hsize, hsize)]
+            attended[here, cols] = (dot_tn(main, value) + dot_tn(rest, value)).astype(BF16)
     pltpu.make_async_copy(relay, relay, relay_recv).wait()
     for turn in range(NEAR):
         onward = along(turn, rings) - halfway(turn, rings) + rings
@@ -360,9 +379,7 @@
         pick[here, :] = onehot(iota((gslots, nodes), 1) + 1 == wanted.astype(jnp.int32))
         mem_s[blocks] = pack(dot(pick[here, :], table[...]))
         send_groups(mem_s, mem_r, 1, g, g + 1)
-    block = LANES
-    scale = 1.0 / jnp.sqrt(jnp.float32(hsize))
-    for b in range(nodes // block):
+    for b in range(2, nodes // block):
         here = pl.ds(b * block, block)
         times = jnp.zeros((nodes, block), F32)
         for j in range(nbr.shape[0]):

time: 75 us -> 75.4 us (level)
  no operation moved by 1% of the time
where the time goes in v4:
time: 75.4 us; the launch traced here: 75.3 us
  Pallas kernels  72.8 us (97%)
  between operations  1.81 us (2%)
    pallas_call x1, Pallas kernels, shards(): pl.pallas_call(functools.partial(kernel, parts, groups), out_shape=(pltpu...  72.8 us

profile of v4, /device:TPU:1, one launch (start us, length us, event | category | flops | bytes accessed | tf_op | source)
XLA Modules:
  0.0 75.3 jit_solution(12951616875665846745)
XLA Ops:
  0.6 72.8 %window.1 = (bf16[512,256]{1,0:T(8,128)(2,1)S(1)}, f32[1,128]{1,0:T(1,128)S(1)}) custom-call(bf16[512,256]{1,0:T(8,128)(2,1)} %bitcast.16, s32[10,512]{1,0:T(8,128)} %bitcast.17, s32[2,128]{1,0:T(2,128)} %bitcast.19, s32[2,128]{1,0:T(2,128)} %bitcast.20, bf16[128,128]{1,0:T(8,128)(2,1)} %bitcast.18, s32[1,128]{1,0:T(1,128)} %lab_h.1, ...), custom_call_target="tpu_custom_call" | custom-call | tf_op jit(solution)/shard_map/window/pallas_call | solution.py:604
  73.4 0.7 copy.22
